TPU v7x, 32 devices: a whole 2x2x4 slice. The times are simulated.
32 devices in a mesh: tm: 4 (over z), row: 4 (over y, core), col: 2 (over x).
Axes of the slice: x: 2, y: 2, z: 4, core: 2. Of those that a mesh axis runs over, the one named last changes fastest.
Arguments:
- frames: float32 [4, 1024, 1024], P('tm', 'row', 'col'), may hold values from 0 to 200, as said below
- following: float32 [1024, 1024], P('row', 'col'), may hold values from 0 to 200, as said below
Outputs:
- planes: float32 [4, 32, 64, 2048], P('tm', 'row', None, 'col')
Inputs may be any that keep to these rules, and one draw needn't show every extreme that they name: `frames`: detector intensities, never negative. `following`: detector intensities, never negative.
All inputs are finite; a program needn't handle non-finite values.
Results may differ from a plain program's by a relative error of at most 0.000071.
Values sent between devices are 32-bit elements; how exact they have to be, the bound alone decides.
A program may use at most 128 MiB of HBM per device.

v0:
```python
import functools

import jax
import jax.numpy as jnp
import ml_dtypes
import numpy as np
from jax import lax
from jax.experimental import pallas as pl
from jax.experimental.pallas import tpu as pltpu
from jax.sharding import PartitionSpec as P

W = 64
HALF = W // 2
STRIDE = 32
LANES = 128
GROUP = 256
PER = GROUP // W
MESH = pl.DeviceIdType.MESH
BF16 = jnp.bfloat16
F32 = jnp.float32


def halves(table):
    high = table.astype(ml_dtypes.bfloat16)
    low = (table - high.astype(np.float64)).astype(ml_dtypes.bfloat16)
    return high, low


def tables():
    angle = 2 * np.pi * (np.outer(np.arange(W), np.arange(HALF + 1)) % W) / W
    cosine, sine = np.cos(angle), np.sin(angle)
    packed = np.concatenate([cosine[:, :HALF], cosine[:, HALF:], sine[:, 1:HALF]], axis=1)
    sign = np.where(np.arange(W) > HALF, -1.0, 1.0)
    weight = np.where(np.arange(W) % HALF == 0, 1.0, 2.0)
    forward_lanes = np.zeros((GROUP, GROUP))
    inverse_lanes = np.zeros((GROUP, GROUP))
    ones = np.zeros((GROUP, GROUP))
    for w in range(PER):
        cells = slice(w * W, w * W + W)
        ones[cells, cells] = 1.0
        for part in range(2):
            slots = slice(part * HALF, part * HALF + HALF)
            place = slice(part * LANES + w * HALF, part * LANES + w * HALF + HALF)
            forward_lanes[cells, place] = (packed * sign)[:, slots]
            inverse_lanes[place, cells] = (packed * weight)[:, slots].T
    square = np.stack(
        [*halves(forward_lanes), *halves(inverse_lanes), ones.astype(ml_dtypes.bfloat16)]
    )
    down, up = packed.T, packed * weight / float(W * W * W)
    tall = []
    for table in (down, up):
        high, low = halves(table)
        tall.append(np.concatenate([high, low, high, low], axis=1))
    return square, np.stack(tall)


def split(x):
    high = x.astype(BF16)
    return high, (x - high.astype(F32)).astype(BF16)


def dot(a, b):
    return jnp.dot(a, b, preferred_element_type=F32)


def expand(block):
    count = block.shape[1] // LANES - 1
    lane = lax.broadcasted_iota(jnp.int32, (W, LANES), 1)
    out = []
    for n in range(count):
        here = block[:, n * LANES : (n + 1) * LANES]
        after = block[:, (n + 1) * LANES : (n + 2) * LANES]
        out.append(jnp.where(lane < W, here, pltpu.roll(here, STRIDE, 1)))
        mixed = jnp.where(lane >= LANES - STRIDE, here, after)
        out.append(
            jnp.where(lane < W, pltpu.roll(here, W, 1), pltpu.roll(mixed, LANES - STRIDE, 1))
        )
    return jnp.concatenate(out, axis=1)


def group_sums(columns, ones):
    groups = columns[0].shape[1] // GROUP
    tall = jnp.concatenate(
        [c[:, g * GROUP : (g + 1) * GROUP] for c in columns for g in range(groups)], axis=0
    )
    high, rest = tall.astype(BF16), None
    rest = tall - high.astype(F32)
    mid, low = split(rest)
    rows = tall.shape[0]
    sums = dot(jnp.concatenate([high, mid, low], axis=0), ones)
    sums = sums[:rows] + sums[rows : 2 * rows] + sums[2 * rows :]
    out = []
    for c in range(len(columns)):
        parts = [sums[(c * groups + g) * 8 : (c * groups + g) * 8 + 8] for g in range(groups)]
        out.append(jnp.sum(jnp.concatenate(parts, axis=1), axis=0, keepdims=True))
    return out


def fold(x):
    return jnp.sum(x.reshape(W // 8, 8, x.shape[1]), axis=0)


def stack_groups(arrays):
    return jnp.concatenate(
        [
            a[:, g * GROUP : (g + 1) * GROUP]
            for a in arrays
            for g in range(a.shape[1] // GROUP)
        ],
        axis=0,
    )


def unstack_groups(tall, count):
    groups = tall.shape[0] // (count * W)
    return [
        jnp.concatenate(
            [tall[(c * groups + g) * W : (c * groups + g + 1) * W] for g in range(groups)], axis=1
        )
        for c in range(count)
    ]


def by_lanes(arrays, high_table, low_table):
    high, low = split(stack_groups(arrays))
    rows = high.shape[0]
    both = dot(jnp.concatenate([high, low], axis=0), high_table)
    tall = both[:rows] + both[rows:] + dot(high, low_table)
    return unstack_groups(tall, len(arrays))


def by_rows(x, table):
    high, low = split(x)
    return dot(table, jnp.concatenate([high, high, low, low], axis=0))


def forward(blocks, square, tall):
    windows = [expand(b) for b in blocks]
    means = group_sums([fold(w) for w in windows], square[4])
    centred = [w - m * (1.0 / (W * W)) for w, m in zip(windows, means)]
    spreads = group_sums([fold(c * c) for c in centred], square[4])
    scales = [lax.rsqrt(s * (1.0 / (W * W)) + 1e-05) for s in spreads]
    rows = by_lanes(centred, square[0], square[1])
    return [by_rows(r, tall[0]) for r in rows], scales


def multiply(x1, x2):
    row = lax.broadcasted_iota(jnp.int32, (HALF, LANES), 0)
    lane = lax.broadcasted_iota(jnp.int32, (HALF, LANES), 1)
    mk = row == 0
    ml = lax.rem(lane, HALF) == 0
    either, both = mk | ml, mk & ml
    top, bottom = [], []
    for g in range(x1.shape[1] // GROUP):
        real, imag = slice(g * GROUP, g * GROUP + LANES), slice(g * GROUP + LANES, (g + 1) * GROUP)
        a1, c1, d1, b1 = x1[:HALF, real], x1[:HALF, imag], x1[HALF:, real], x1[HALF:, imag]
        a2, c2, d2, b2 = x2[:HALF, real], x2[:HALF, imag], x2[HALF:, real], x2[HALF:, imag]
        bb, cc, dd = b1 * b2, c1 * c2, d1 * d2
        cb_bc, bd_db = c1 * b2 - b1 * c2, b1 * d2 - d1 * b2
        top.append(
            a1 * a2 + jnp.where(ml, 0.0, cc) + jnp.where(mk, 0.0, dd) + jnp.where(either, 0.0, bb)
        )
        top.append(
            jnp.where(ml, cc, c1 * a2 - a1 * c2) + jnp.where(mk, 0.0, jnp.where(ml, bb, bd_db))
        )
        bottom.append(
            jnp.where(mk, dd, a1 * d2 - d1 * a2) + jnp.where(ml, 0.0, jnp.where(mk, bb, cb_bc))
        )
        inner = c1 * d2 + d1 * c2 - a1 * b2 - b1 * a2
        bottom.append(
            jnp.where(both, bb, jnp.where(ml, cb_bc, jnp.where(mk, bd_db, inner)))
        )
    return jnp.concatenate(
        [jnp.concatenate(top, axis=1), jnp.concatenate(bottom, axis=1)], axis=0
    )


def inverse(powers, square, tall):
    return by_lanes([by_rows(p, tall[1]) for p in powers], square[2], square[3])


def kernel(
    sizes, frames, following, square_in, tall_in, out,
    ext, spec, scale, result, square, tall, local_sem, send_sem, recv_sem, out_sem,
):
    F, H, B = frames.shape
    rows = H // STRIDE
    pairs = rows // 2
    tm, row, col = (lax.axis_index(a) for a in ("tm", "row", "col"))
    last_tm, last_row, last_col = (s - 1 for s in sizes)
    has_next, has_prev = tm < last_tm, tm > 0
    has_below, has_above = row < last_row, row > 0
    has_right, has_left = col < last_col, col > 0
    up, left, back = (jnp.maximum(v - 1, 0) for v in (row, col, tm))
    down, right, ahead = (
        jnp.minimum(v + 1, s) for v, s in ((row, last_row), (col, last_col), (tm, last_tm))
    )

    own = pltpu.make_async_copy(frames, ext.at[pl.ds(0, F), pl.ds(0, H), pl.ds(0, B)], local_sem.at[0])
    own.start()
    after = pltpu.make_async_copy(following, ext.at[F, pl.ds(0, H), pl.ds(0, B)], local_sem.at[1])
    pl.when(~has_next)(after.start)
    load_square = pltpu.make_async_copy(square_in, square, local_sem.at[2])
    load_square.start()
    load_tall = pltpu.make_async_copy(tall_in, tall, local_sem.at[3])
    load_tall.start()

    neighbours = [
        (has_prev, (back, row, col)),
        (has_next, (ahead, row, col)),
        (has_above, (tm, up, col)),
        (has_below, (tm, down, col)),
        (has_left, (tm, row, left)),
        (has_right, (tm, row, right)),
        (has_above & has_left, (tm, up, left)),
        (has_below & has_right, (tm, down, right)),
    ]
    barrier = pltpu.get_barrier_semaphore()
    for there, device in neighbours:
        @pl.when(there)
        def _(device=device):
            pl.semaphore_signal(barrier, inc=1, device_id=device, device_id_type=MESH)
    pl.semaphore_wait(barrier, sum(there.astype(jnp.int32) for there, _ in neighbours))

    def remote(source, target, number, device):
        return pltpu.make_async_remote_copy(
            src_ref=source, dst_ref=target, send_sem=send_sem.at[number],
            recv_sem=recv_sem.at[number], device_id=device, device_id_type=MESH,
        )

    strip = remote(
        frames.at[0, :, pl.ds(0, LANES)], ext.at[F, pl.ds(0, H), pl.ds(0, LANES)], 0, (back, row, col)
    )
    edges = [0, STRIDE] + [STRIDE + W * (p + 1) for p in range(pairs - 1)] + [H]
    wide = pl.ds(LANES, B - LANES)
    bands = [
        remote(
            frames.at[0, pl.ds(lo, hi - lo), wide], ext.at[F, pl.ds(lo, hi - lo), wide],
            1 + n, (back, row, col),
        )
        for n, (lo, hi) in enumerate(zip(edges[:-1], edges[1:]))
    ]
    base = 1 + len(bands)
    rim_rows, rim_cols = pl.ds(H, STRIDE), pl.ds(B, LANES)
    first, everyone = pl.ds(0, LANES), pl.ds(0, F)
    rims = [
        (has_left, has_right, remote(
            frames.at[:, :, first], ext.at[everyone, pl.ds(0, H), rim_cols],
            base, (tm, row, left))),
        (has_above, has_below, remote(
            frames.at[:, pl.ds(0, STRIDE), :], ext.at[everyone, rim_rows, pl.ds(0, B)],
            base + 1, (tm, up, col))),
        (has_above & has_left, has_below & has_right, remote(
            frames.at[:, pl.ds(0, STRIDE), first], ext.at[everyone, rim_rows, rim_cols],
            base + 2, (tm, up, left))),
    ]
    late = [
        (has_left, has_right, remote(
            ext.at[F, pl.ds(0, H), first], ext.at[F, pl.ds(0, H), rim_cols],
            base + 3, (tm, row, left))),
        (has_above & has_left, has_below & has_right, remote(
            ext.at[F, pl.ds(0, STRIDE), first], ext.at[F, rim_rows, rim_cols],
            base + 4, (tm, up, left))),
        (has_above, has_below, remote(
            ext.at[F, pl.ds(0, STRIDE), pl.ds(0, B)], ext.at[F, rim_rows, pl.ds(0, B)],
            base + 5, (tm, up, col))),
    ]

    @pl.when(has_prev)
    def _():
        strip.start()
        for band in bands:
            band.start()
    for sends, _, copy in rims:
        pl.when(sends)(copy.start)

    @pl.when(~has_right)
    def _():
        ext[:, :, pl.ds(B, LANES)] = jnp.zeros((F + 1, H + STRIDE, LANES), F32)

    @pl.when(~has_below)
    def _():
        ext[:, pl.ds(H, STRIDE), :] = jnp.zeros((F + 1, STRIDE, B + LANES), F32)

    load_square.wait()
    load_tall.wait()
    own.wait()
    for _, comes, copy in rims:
        pl.when(comes)(copy.wait_recv)

    def spectra(frame, p):
        blocks = []
        for r in range(2):
            start = pl.multiple_of((2 * p + r) * STRIDE, STRIDE)
            blocks.append(ext[frame, pl.ds(start, W), :])
        return forward(blocks, square, tall)

    def keep(slot, p, found):
        for r in range(2):
            spec[slot, 2 * p + r] = found[0][r]
            scale[slot, 2 * p + r] = jnp.broadcast_to(found[1][r], scale.shape[2:])

    def emit(frame, slot, p, found):
        powers = [multiply(spec[slot, 2 * p + r], found[0][r]) for r in range(2)]
        planes = inverse(powers, square, tall)
        for r in range(2):
            factor = found[1][r] * scale[slot, 2 * p + r][:1]
            result[frame, 2 * p + r] = planes[r] * factor

    def to_out(frame, p):
        part = pl.ds(2 * p, 2)
        return pltpu.make_async_copy(
            result.at[frame, part], out.at[frame, part], out_sem.at[frame, p]
        )

    @pl.loop(0, pairs)
    def _(p):
        keep(0, p, spectra(0, p))

    for f in range(1, F):
        @pl.loop(0, pairs)
        def _(p):
            found = spectra(f, p)
            emit(f - 1, (f - 1) % 2, p, found)
            keep(f % 2, p, found)
            to_out(f - 1, p).start()

    @pl.when(has_next)
    def _():
        strip.wait_recv()
        bands[0].wait_recv()

    pl.when(~has_next)(after.wait)
    for sends, _, copy in late:
        pl.when(sends)(copy.start)
    for _, comes, copy in late[:1]:
        pl.when(comes)(copy.wait_recv)
    for p in range(pairs):
        pl.when(has_next)(bands[p + 1].wait_recv)
        if p == pairs - 1:
            for _, comes, copy in late[1:]:
                pl.when(comes)(copy.wait_recv)
        emit(F - 1, (F - 1) % 2, p, spectra(F, p))
        to_out(F - 1, p).start()

    @pl.when(has_prev)
    def _():
        strip.wait_send()
        for band in bands:
            band.wait_send()
    for sends, _, copy in rims + late:
        pl.when(sends)(copy.wait_send)
    for f in range(F):
        for p in range(pairs):
            to_out(f, p).wait()


def on_device(sizes, frames, following):
    F, H, B = frames.shape
    rows, lanes = H // STRIDE, B // STRIDE * W
    square, tall = tables()
    copies = 1 + rows // 2 + 1 + 6
    return pl.pallas_call(
        functools.partial(kernel, sizes),
        out_shape=jax.ShapeDtypeStruct((F, rows, W, lanes), F32),
        in_specs=[pl.BlockSpec(memory_space=pl.ANY)] * 4,
        out_specs=pl.BlockSpec(memory_space=pl.ANY),
        scratch_shapes=[
            pltpu.VMEM((F + 1, H + STRIDE, B + LANES), F32),
            pltpu.VMEM((2, rows, W, lanes), F32),
            pltpu.VMEM((2, rows, 8, lanes), F32),
            pltpu.VMEM((F, rows, W, lanes), F32),
            pltpu.VMEM(square.shape, BF16),
            pltpu.VMEM(tall.shape, BF16),
            pltpu.SemaphoreType.DMA((4,)),
            pltpu.SemaphoreType.DMA((copies,)),
            pltpu.SemaphoreType.DMA((copies,)),
            pltpu.SemaphoreType.DMA((F, rows // 2)),
        ],
        compiler_params=pltpu.CompilerParams(
            collective_id=0, has_side_effects=True, vmem_limit_bytes=40 * 1024 * 1024
        ),
    )(frames, following, jnp.asarray(square), jnp.asarray(tall))


def solution(mesh):
    sizes = tuple(mesh.shape[a] for a in ("tm", "row", "col"))
    return jax.shard_map(
        functools.partial(on_device, sizes),
        mesh=mesh,
        in_specs=(P("tm", "row", "col"), P("row", "col")),
        out_specs=P("tm", "row", None, "col"),
        check_vma=False,
    )
```

profile of v0, /device:TPU:1, one launch (start us, length us, event | category | flops | bytes accessed | tf_op | source)
XLA Modules:
  0.0 29.1 jit_solution(502261057452780162)
XLA Ops:
  0.0 0.0 copy-start
  0.0 1.1 %copy-done = bf16[5,256,256]{2,1,0:T(8,128)(2,1)S(1)} copy-done((bf16[5,256,256]{2,1,0:T(8,128)(2,1)S(1)}, bf16[5,256,256]{2,1,0:T(8,128)(2,1)}, u32[]{:S(2)}) %copy-start) | copy-done | bytes 655384
  1.1 0.0 copy-start.1
  1.1 1.0 %copy-done.1 = f32[1,256,512]{2,1,0:T(8,128)S(1)} copy-done((f32[1,256,512]{2,1,0:T(8,128)S(1)}, f32[1,256,512]{2,1,0:T(8,128)}, u32[]{:S(2)}) %copy-start.1) | copy-done | bytes 524312
  2.1 0.0 copy-start.2
  2.1 1.0 %copy-done.2 = f32[256,512]{1,0:T(8,128)S(1)} copy-done((f32[256,512]{1,0:T(8,128)S(1)}, f32[256,512]{1,0:T(8,128)}, u32[]{:S(2)}) %copy-start.2) | copy-done | bytes 524312
  3.2 0.0 copy-start.3
  3.2 0.8 %copy-done.3 = bf16[2,64,256]{2,1,0:T(8,128)(2,1)S(1)} copy-done((bf16[2,64,256]{2,1,0:T(8,128)(2,1)S(1)}, bf16[2,64,256]{2,1,0:T(8,128)(2,1)}, u32[]{:S(2)}) %copy-start.3) | copy-done | bytes 65560
  4.0 23.7 %shard_map.46 = f32[1,8,64,1024]{3,2,1,0:T(8,128)S(1)} custom-call(f32[1,256,512]{2,1,0:T(8,128)S(1)} %copy-done.1, f32[256,512]{1,0:T(8,128)S(1)} %copy-done.2, bf16[5,256,256]{2,1,0:T(8,128)(2,1)S(1)} %copy-done, bf16[2,64,256]{2,1,0:T(8,128)(2,1)S(1)} %copy-done.3), custom_call_target="tpu_custom_call" | custom-call | tf_op jit(solution)/shard_map/pallas_call | solution.py:363
  27.8 1.3 %copy.6 = f32[1,8,64,1024]{3,2,1,0:T(8,128)} copy(f32[1,8,64,1024]{3,2,1,0:T(8,128)S(1)} %shard_map.46) | data formatting | bytes 4194304
Async XLA Ops:
  0.0 1.1 %copy-start = (bf16[5,256,256]{2,1,0:T(8,128)(2,1)S(1)}, bf16[5,256,256]{2,1,0:T(8,128)(2,1)}, u32[]{:S(2)}) copy-start(bf16[5,256,256]{2,1,0:T(8,128)(2,1)} %constant.4.clone.square_in) | copy-start | bytes 1966084
  1.1 1.0 %copy-start.1 = (f32[1,256,512]{2,1,0:T(8,128)S(1)}, f32[1,256,512]{2,1,0:T(8,128)}, u32[]{:S(2)}) copy-start(f32[1,256,512]{2,1,0:T(8,128)} %frames.1) | copy-start | bytes 1572868
  2.1 1.0 %copy-start.2 = (f32[256,512]{1,0:T(8,128)S(1)}, f32[256,512]{1,0:T(8,128)}, u32[]{:S(2)}) copy-start(f32[256,512]{1,0:T(8,128)} %following.1) | copy-start | bytes 1572868
  3.2 0.8 %copy-start.3 = (bf16[2,64,256]{2,1,0:T(8,128)(2,1)S(1)}, bf16[2,64,256]{2,1,0:T(8,128)(2,1)}, u32[]{:S(2)}) copy-start(bf16[2,64,256]{2,1,0:T(8,128)(2,1)} %constant.5.clone.tall_in) | copy-start | bytes 196612
where the time goes:
time: 29.4 us; the launch traced here: 29.1 us
  Pallas kernels  23.7 us (81%)
  local copies, waits for them, and re-layouts  5.33 us (18%)
    pallas_call x1, Pallas kernels, on_device(): pl.pallas_call(functools.partial(kernel, sizes), out_shape=jax.ShapeDtype...  23.7 us
    unnamed x9, local copies, waits for them, and re-layouts  5.33 us

commit v1 on v0

--- a/solution.py
+++ b/solution.py
@@ -15,6 +15,7 @@
 LANES = 128
 GROUP = 256
 PER = GROUP // W
+DEPTH = 2
 MESH = pl.DeviceIdType.MESH
 BF16 = jnp.bfloat16
 F32 = jnp.float32
@@ -63,6 +64,27 @@
     return jnp.dot(a, b, preferred_element_type=F32)
 
 
+def pack(columns):
+    lane = lax.broadcasted_iota(jnp.int32, (8, LANES), 1)
+    out = []
+    for top in range(0, columns.shape[0], STRIDE):
+        tiles = [columns[top + 8 * b : top + 8 * b + 8] for b in range(4)]
+        tile = tiles[0]
+        for b in range(1, 4):
+            tile = jnp.where(lane < b * STRIDE, tile, pltpu.roll(tiles[b], b * STRIDE, 1))
+        out.append(tile)
+    return jnp.concatenate(out, axis=0)
+
+
+def unpack(packed):
+    out = []
+    for top in range(0, packed.shape[0], 8):
+        tile = packed[top : top + 8]
+        out.append(tile)
+        out += [pltpu.roll(tile, LANES - b * STRIDE, 1) for b in range(1, 4)]
+    return jnp.concatenate(out, axis=0)
+
+
 def expand(block):
     count = block.shape[1] // LANES - 1
     lane = lax.broadcasted_iota(jnp.int32, (W, LANES), 1)
@@ -181,7 +203,7 @@
 
 def kernel(
     sizes, frames, following, square_in, tall_in, out,
-    ext, spec, scale, result, square, tall, local_sem, send_sem, recv_sem, out_sem,
+    ext, rim, packed, spec, scale, result, square, tall, local_sem, send_sem, recv_sem, out_sem,
 ):
     F, H, B = frames.shape
     rows = H // STRIDE
@@ -208,6 +230,10 @@
     neighbours = [
         (has_prev, (back, row, col)),
         (has_next, (ahead, row, col)),
+        (has_prev & has_left, (back, row, left)),
+        (has_next & has_right, (ahead, row, right)),
+        (has_prev & has_above & has_left, (back, up, left)),
+        (has_next & has_below & has_right, (ahead, down, right)),
         (has_above, (tm, up, col)),
         (has_below, (tm, down, col)),
         (has_left, (tm, row, left)),
@@ -228,71 +254,80 @@
             recv_sem=recv_sem.at[number], device_id=device, device_id_type=MESH,
         )
 
-    strip = remote(
-        frames.at[0, :, pl.ds(0, LANES)], ext.at[F, pl.ds(0, H), pl.ds(0, LANES)], 0, (back, row, col)
-    )
     edges = [0, STRIDE] + [STRIDE + W * (p + 1) for p in range(pairs - 1)] + [H]
-    wide = pl.ds(LANES, B - LANES)
     bands = [
         remote(
-            frames.at[0, pl.ds(lo, hi - lo), wide], ext.at[F, pl.ds(lo, hi - lo), wide],
-            1 + n, (back, row, col),
+            frames.at[0, pl.ds(lo, hi - lo)], ext.at[F, pl.ds(lo, hi - lo)], n, (back, row, col)
         )
         for n, (lo, hi) in enumerate(zip(edges[:-1], edges[1:]))
     ]
-    base = 1 + len(bands)
-    rim_rows, rim_cols = pl.ds(H, STRIDE), pl.ds(B, LANES)
-    first, everyone = pl.ds(0, LANES), pl.ds(0, F)
-    rims = [
-        (has_left, has_right, remote(
-            frames.at[:, :, first], ext.at[everyone, pl.ds(0, H), rim_cols],
-            base, (tm, row, left))),
-        (has_above, has_below, remote(
-            frames.at[:, pl.ds(0, STRIDE), :], ext.at[everyone, rim_rows, pl.ds(0, B)],
-            base + 1, (tm, up, col))),
-        (has_above & has_left, has_below & has_right, remote(
-            frames.at[:, pl.ds(0, STRIDE), first], ext.at[everyone, rim_rows, rim_cols],
-            base + 2, (tm, up, left))),
+    base = len(bands)
+    quarter = H // 4
+    cells, corner, head = pl.ds(0, quarter), pl.ds(quarter, 8), pl.ds(0, 8)
+    mine = pl.ds(0, F)
+    below = remote(frames.at[:, pl.ds(0, STRIDE), :], ext.at[mine, pl.ds(H, STRIDE)], base, (tm, up, col))
+    below_late = remote(ext.at[F, pl.ds(0, STRIDE)], ext.at[F, pl.ds(H, STRIDE)], base + 1, (tm, up, col))
+    to_side = remote(packed.at[mine], rim.at[mine, cells], base + 2, (tm, row, left))
+    to_corner = remote(packed.at[mine, head], rim.at[mine, corner], base + 3, (tm, up, left))
+    side_back = remote(packed.at[0], rim.at[F, cells], base + 4, (back, row, left))
+    corner_back = remote(packed.at[0, head], rim.at[F, corner], base + 5, (back, up, left))
+    side_end = remote(packed.at[F], rim.at[F, cells], base + 4, (tm, row, left))
+    corner_end = remote(packed.at[F, head], rim.at[F, corner], base + 5, (tm, up, left))
+    diagonal = has_above & has_left
+    sides = [
+        (has_left, to_side),
+        (diagonal, to_corner),
+        (has_left & has_prev, side_back),
+        (diagonal & has_prev, corner_back),
     ]
-    late = [
-        (has_left, has_right, remote(
-            ext.at[F, pl.ds(0, H), first], ext.at[F, pl.ds(0, H), rim_cols],
-            base + 3, (tm, row, left))),
-        (has_above & has_left, has_below & has_right, remote(
-            ext.at[F, pl.ds(0, STRIDE), first], ext.at[F, rim_rows, rim_cols],
-            base + 4, (tm, up, left))),
-        (has_above, has_below, remote(
-            ext.at[F, pl.ds(0, STRIDE), pl.ds(0, B)], ext.at[F, rim_rows, pl.ds(0, B)],
-            base + 5, (tm, up, col))),
-    ]
+    ends = [(has_left & ~has_next, side_end), (diagonal & ~has_next, corner_end)]
 
     @pl.when(has_prev)
     def _():
-        strip.start()
-        for band in bands:
+        for band in bands[:DEPTH]:
             band.start()
-    for sends, _, copy in rims:
-        pl.when(sends)(copy.start)
+    pl.when(has_above)(below.start)
+
+    own.wait()
+    for f in range(F):
+        packed[f] = pack(ext[f, pl.ds(0, H), pl.ds(0, LANES)])
+    for goes, copy in sides:
+        pl.when(goes)(copy.start)
+
+    @pl.when(~has_next)
+    def _():
+        after.wait()
+        packed[F] = pack(ext[F, pl.ds(0, H), pl.ds(0, LANES)])
+    for goes, copy in ends:
+        pl.when(goes)(copy.start)
+    @pl.when(has_prev)
+    def _():
+        for band in bands[DEPTH:]:
+            band.start()
 
     @pl.when(~has_right)
     def _():
-        ext[:, :, pl.ds(B, LANES)] = jnp.zeros((F + 1, H + STRIDE, LANES), F32)
+        rim[...] = jnp.zeros(rim.shape, F32)
 
     @pl.when(~has_below)
     def _():
-        ext[:, pl.ds(H, STRIDE), :] = jnp.zeros((F + 1, STRIDE, B + LANES), F32)
+        ext[:, pl.ds(H, STRIDE), :] = jnp.zeros((F + 1, STRIDE, B), F32)
+        rim[:, corner, :] = jnp.zeros((F + 1, 8, LANES), F32)
 
     load_square.wait()
     load_tall.wait()
-    own.wait()
-    for _, comes, copy in rims:
-        pl.when(comes)(copy.wait_recv)
+    pl.when(has_below)(below.wait_recv)
+    pl.when(has_right)(to_side.wait_recv)
+    pl.when(has_right & has_below)(to_corner.wait_recv)
 
     def spectra(frame, p):
         blocks = []
         for r in range(2):
             start = pl.multiple_of((2 * p + r) * STRIDE, STRIDE)
-            blocks.append(ext[frame, pl.ds(start, W), :])
+            tiles = pl.ds(pl.multiple_of((2 * p + r) * 8, 8), 16)
+            blocks.append(
+                jnp.concatenate([ext[frame, pl.ds(start, W), :], unpack(rim[frame, tiles])], axis=1)
+            )
         return forward(blocks, square, tall)
 
     def keep(slot, p, found):
@@ -313,8 +348,7 @@
             result.at[frame, part], out.at[frame, part], out_sem.at[frame, p]
         )
 
-    @pl.loop(0, pairs)
-    def _(p):
+    for p in range(pairs):
         keep(0, p, spectra(0, p))
 
     for f in range(1, F):
@@ -325,31 +359,25 @@
             keep(f % 2, p, found)
             to_out(f - 1, p).start()
 
-    @pl.when(has_next)
-    def _():
-        strip.wait_recv()
-        bands[0].wait_recv()
-
-    pl.when(~has_next)(after.wait)
-    for sends, _, copy in late:
-        pl.when(sends)(copy.start)
-    for _, comes, copy in late[:1]:
-        pl.when(comes)(copy.wait_recv)
+    pl.when(has_next)(bands[0].wait_recv)
+    pl.when(has_above)(below_late.start)
+    pl.when(has_right)(side_back.wait_recv)
     for p in range(pairs):
         pl.when(has_next)(bands[p + 1].wait_recv)
         if p == pairs - 1:
-            for _, comes, copy in late[1:]:
-                pl.when(comes)(copy.wait_recv)
+            pl.when(has_below)(below_late.wait_recv)
+            pl.when(has_right & has_below)(corner_back.wait_recv)
         emit(F - 1, (F - 1) % 2, p, spectra(F, p))
         to_out(F - 1, p).start()
 
     @pl.when(has_prev)
     def _():
-        strip.wait_send()
         for band in bands:
             band.wait_send()
-    for sends, _, copy in rims + late:
-        pl.when(sends)(copy.wait_send)
+    pl.when(has_above)(below.wait_send)
+    pl.when(has_above)(below_late.wait_send)
+    for goes, copy in sides + ends:
+        pl.when(goes)(copy.wait_send)
     for f in range(F):
         for p in range(pairs):
             to_out(f, p).wait()
@@ -366,7 +394,9 @@
         in_specs=[pl.BlockSpec(memory_space=pl.ANY)] * 4,
         out_specs=pl.BlockSpec(memory_space=pl.ANY),
         scratch_shapes=[
-            pltpu.VMEM((F + 1, H + STRIDE, B + LANES), F32),
+            pltpu.VMEM((F + 1, H + STRIDE, B), F32),
+            pltpu.VMEM((F + 1, H // 4 + 8, LANES), F32),
+            pltpu.VMEM((F + 1, H // 4, LANES), F32),
             pltpu.VMEM((2, rows, W, lanes), F32),
             pltpu.VMEM((2, rows, 8, lanes), F32),
             pltpu.VMEM((F, rows, W, lanes), F32),
@@ -378,7 +408,7 @@
             pltpu.SemaphoreType.DMA((F, rows // 2)),
         ],
         compiler_params=pltpu.CompilerParams(
-            collective_id=0, has_side_effects=True, vmem_limit_bytes=40 * 1024 * 1024
+            collective_id=0, has_side_effects=True, vmem_limit_bytes=60 * 1024 * 1024
         ),
     )(frames, following, jnp.asarray(square), jnp.asarray(tall))
 

time: 29.4 us -> 25.3 us (0.86)
  local copies, waits for them, and re-layouts: 5.33 us -> 3.16 us
  Pallas kernels: 23.7 us -> 22 us
    unnamed x9 -> x1, local copies, waits for them, and re-layouts: 5.33 us -> 3.16 us
    pallas_call x1, Pallas kernels: 23.7 us -> 22 us  [on_device(): pl.pallas_call(functools.partial(kernel, sizes), out_shape=jax.ShapeDtype...]
where the time goes in v1:
time: 25.3 us; the launch traced here: 25.2 us
  Pallas kernels  22 us (87%)
  local copies, waits for them, and re-layouts  3.16 us (12%)
    pallas_call x1, Pallas kernels, on_device(): pl.pallas_call(functools.partial(kernel, sizes), out_shape=jax.ShapeDtype...  22 us
    unnamed x1, local copies, waits for them, and re-layouts  3.16 us

profile of v1, /device:TPU:1, one launch (start us, length us, event | category | flops | bytes accessed | tf_op | source)
XLA Modules:
  0.0 25.2 jit_solution(856157773627275213)
XLA Ops:
  0.0 22.0 %shard_map.46 = f32[1,8,64,1024]{3,2,1,0:T(8,128)} custom-call(f32[1,256,512]{2,1,0:T(8,128)} %frames.1, f32[256,512]{1,0:T(8,128)} %following.1, bf16[5,256,256]{2,1,0:T(8,128)(2,1)} %constant.4.clone.square_in, bf16[2,64,256]{2,1,0:T(8,128)(2,1)} %constant.5.clone.tall_in), custom_call_target="tpu_custom_call" | custom-call | tf_op jit(solution)/shard_map/pallas_call | solution.py:391
  22.0 3.2 %copy.6 = f32[1,8,64,1024]{3,2,1,0:T(8,128)} copy(f32[1,8,64,1024]{3,2,1,0:T(8,128)} %shard_map.46) | data formatting | bytes 4194304

commit v2 on v1

--- a/solution.py
+++ b/solution.py
@@ -390,7 +390,7 @@
     copies = 1 + rows // 2 + 1 + 6
     return pl.pallas_call(
         functools.partial(kernel, sizes),
-        out_shape=jax.ShapeDtypeStruct((F, rows, W, lanes), F32),
+        out_shape=pltpu.VMEM((F, rows, W, lanes), F32),
         in_specs=[pl.BlockSpec(memory_space=pl.ANY)] * 4,
         out_specs=pl.BlockSpec(memory_space=pl.ANY),
         scratch_shapes=[
@@ -408,7 +408,7 @@
             pltpu.SemaphoreType.DMA((F, rows // 2)),
         ],
         compiler_params=pltpu.CompilerParams(
-            collective_id=0, has_side_effects=True, vmem_limit_bytes=60 * 1024 * 1024
+            collective_id=0, has_side_effects=True, vmem_limit_bytes=58 * 1024 * 1024
         ),
     )(frames, following, jnp.asarray(square), jnp.asarray(tall))
 

time: 25.3 us -> 22.8 us (0.901)
  local copies, waits for them, and re-layouts: 3.16 us -> 1.32 us
  Pallas kernels: 22 us -> 21.3 us
    unnamed x1, local copies, waits for them, and re-layouts: 3.16 us -> 1.32 us
    pallas_call x1, Pallas kernels: 22 us -> 21.3 us  [on_device(): pl.pallas_call(functools.partial(kernel, sizes), out_shape=pltpu.VMEM((F,...]
where the time goes in v2:
time: 22.8 us; the launch traced here: 22.6 us
  Pallas kernels  21.3 us (93%)
  local copies, waits for them, and re-layouts  1.32 us (6%)
    pallas_call x1, Pallas kernels, on_device(): pl.pallas_call(functools.partial(kernel, sizes), out_shape=pltpu.VMEM((F,...  21.3 us
    unnamed x1, local copies, waits for them, and re-layouts  1.32 us

profile of v2, /device:TPU:1, one launch (start us, length us, event | category | flops | bytes accessed | tf_op | source)
XLA Modules:
  0.0 22.6 jit_solution(2921351796641139735)
XLA Ops:
  0.0 21.3 %shard_map.46 = f32[1,8,64,1024]{3,2,1,0:T(8,128)S(1)} custom-call(f32[1,256,512]{2,1,0:T(8,128)} %frames.1, f32[256,512]{1,0:T(8,128)} %following.1, bf16[5,256,256]{2,1,0:T(8,128)(2,1)} %constant.4.clone.square_in, bf16[2,64,256]{2,1,0:T(8,128)(2,1)} %constant.5.clone.tall_in), custom_call_target="tpu_custom_call" | custom-call | tf_op jit(solution)/shard_map/pallas_call | solution.py:391
  21.3 1.3 %copy.6 = f32[1,8,64,1024]{3,2,1,0:T(8,128)} copy(f32[1,8,64,1024]{3,2,1,0:T(8,128)S(1)} %shard_map.46) | data formatting | bytes 4194304
